TPU v7x, 32 devices: a whole 2x2x4 slice. The times are simulated.
32 devices in a mesh: dp: 16 (over z, y, x), mp: 2 (over core).
Axes of the slice: x: 2, y: 2, z: 4, core: 2. Of those that a mesh axis runs over, the one named last changes fastest.
Arguments:
- layer_input: bfloat16 [8192, 768], P(('dp', 'mp')), may hold values from -6 to 6
- upstream_grad: bfloat16 [8192, 768], P(('dp', 'mp')), may hold values from -6 to 6
- doc_lengths: int32 [16, 4], P('dp'), may hold values from 1 to 509, as said below
- qkv_weight: float32 [3, 768, 768], P(None, ('mp', 'dp')), may hold values from -0.21875 to 0.21875
- out_weight: float32 [768, 768], P(('mp', 'dp')), may hold values from -0.875 to 0.875
- gate_weight: float32 [3072, 768], P(('mp', 'dp')), may hold values from -0.21875 to 0.21875
- up_weight: float32 [3072, 768], P(('mp', 'dp')), may hold values from -0.21875 to 0.21875
- down_weight: float32 [3072, 768], P(('mp', 'dp')), may hold values from -0.109375 to 0.109375
- qkv_momentum: float32 [3, 768, 768], P(None, ('mp', 'dp')), may hold values from -271.529 to 271.529
- out_momentum: float32 [768, 768], P(('mp', 'dp')), may hold values from -271.529 to 271.529
- gate_momentum: float32 [3072, 768], P(('mp', 'dp')), may hold values from -271.529 to 271.529
- up_momentum: float32 [3072, 768], P(('mp', 'dp')), may hold values from -271.529 to 271.529
- down_momentum: float32 [3072, 768], P(('mp', 'dp')), may hold values from -271.529 to 271.529
- norm_gains: float32 [2, 768], P(None, 'dp'), may hold values from 0.5 to 1.5
- norm_biases: float32 [2, 768], P(None, 'dp'), may hold values from -3 to 3
- adam_first: float32 [4, 768], P(None, 'dp'), may hold values from -56 to 56
- adam_second: float32 [4, 768], P(None, 'dp'), may hold values from 245.76 to 983.04
Outputs:
- mixed: bfloat16 [8192, 768], P(('dp', 'mp'))
- input_grad: float32 [8192, 768], P(('dp', 'mp'))
- qkv_updated: float32 [3, 768, 768], P(None, ('mp', 'dp'))
- out_updated: float32 [768, 768], P(('mp', 'dp'))
- gate_updated: float32 [3072, 768], P(('mp', 'dp'))
- up_updated: float32 [3072, 768], P(('mp', 'dp'))
- down_updated: float32 [3072, 768], P(('mp', 'dp'))
- qkv_carried: float32 [3, 768, 768], P(None, ('mp', 'dp'))
- out_carried: float32 [768, 768], P(('mp', 'dp'))
- gate_carried: float32 [3072, 768], P(('mp', 'dp'))
- up_carried: float32 [3072, 768], P(('mp', 'dp'))
- down_carried: float32 [3072, 768], P(('mp', 'dp'))
- norm_updated: float32 [4, 768], P(None, 'dp')
- norm_first: float32 [4, 768], P(None, 'dp')
- norm_second: float32 [4, 768], P(None, 'dp')
Inputs may be any that keep to these rules, and one draw needn't show every extreme that they name: `doc_lengths`: row p lists the lengths of the 4 documents packed from the first slot of packed sequence p; a row sums to at most 512, the last row to exactly 512 with its first document 512 - 3 long; the remaining slots are padding.
All inputs are finite; a program needn't handle non-finite values.
Results may differ from a plain program's by a relative error of at most 0.035.
Values may be sent and summed in bfloat16 or wider, within the bound.
No kernel may reach another device: no remote copies, remote signals or barrier semaphores. Data moves between devices by JAX's collectives and lax.ppermute only.
A program may use at most 192 MiB of HBM per device.

v0:
```python
import math

import jax
import jax.numpy as jnp
from jax import lax
from jax.sharding import PartitionSpec as P

D = 768
HD = 64
FF = 3072
ORTHO_STEPS = 5
STEP_COUNT = 10


NORM_EPSILON = 1e-12
ROPE_BASE = 1000.0
SCHULZ_LINEAR = 3.4445
SCHULZ_CUBIC = -4.775
SCHULZ_QUINTIC = 2.0315
MOMENTUM_KEEP = 0.5
ORTHO_RATE = 0.2
WEIGHT_DECAY = 0.01
ADAM_RATE = 0.2
BETA_FIRST = 0.9
BETA_SECOND = 0.95
ADAM_EPSILON = 1e-08


def in_blocks(array, dim, length):
    shape = array.shape
    pieces = array.reshape(*shape[:dim], length, shape[dim] // length, *shape[dim + 1 :])
    return jnp.moveaxis(pieces, dim, 0)


def sum_at_owner(array, axis, dim):
    pieces = in_blocks(array, dim, lax.axis_size(axis))
    arrived = lax.all_to_all(pieces, axis, split_axis=0, concat_axis=0, tiled=True)
    return arrived.astype(jnp.float32).sum(axis=0)


def in_one_piece(arrays, axis, dim, along):
    widths = [a.shape[along] for a in arrays]
    both = jnp.concatenate(arrays, axis=along)
    whole = sum_at_owner(both, axis, dim)
    return tuple(jnp.split(whole, [sum(widths[:k]) for k in range(1, len(widths))], axis=along))


def document_layout(lengths, total_rows):
    ends = jnp.cumsum(lengths)
    starts = ends - lengths
    row_ids = jnp.arange(total_rows, dtype=jnp.int32)
    segments = jnp.sum((row_ids[:, None] >= ends[None, :]).astype(jnp.int32), axis=1)
    used_rows = ends[-1]
    matches = segments[:, None] == jnp.arange(lengths.shape[0], dtype=jnp.int32)[None, :]
    anchor = jnp.sum(jnp.where(matches, starts[None, :], 0), axis=1)
    anchor = anchor + jnp.where(segments == lengths.shape[0], used_rows, 0)
    positions = row_ids - anchor
    validity = (row_ids < used_rows).astype(jnp.float32)
    return (segments, positions, validity)


def rotary_tables(positions):
    half_width = HD // 2
    exponents = jnp.arange(half_width, dtype=jnp.float32) * (2.0 / HD)
    frequency = jnp.power(jnp.float32(ROPE_BASE), -exponents)
    angles = positions.astype(jnp.float32)[:, None] * frequency[None, :]
    return (jnp.cos(angles), jnp.sin(angles))


def rotate(vectors, cosine_table, sine_table):
    half_width = vectors.shape[-1] // 2
    leading = vectors[..., :half_width]
    trailing = vectors[..., half_width:]
    cosine_part = cosine_table[:, None, :]
    sine_part = sine_table[:, None, :]
    return jnp.concatenate(
        [
            leading * cosine_part - trailing * sine_part,
            trailing * cosine_part + leading * sine_part,
        ],
        axis=-1,
    )


def unrotate(gradients, cosine_table, sine_table):
    half_width = gradients.shape[-1] // 2
    leading = gradients[..., :half_width]
    trailing = gradients[..., half_width:]
    cosine_part = cosine_table[:, None, :]
    sine_part = sine_table[:, None, :]
    return jnp.concatenate(
        [
            leading * cosine_part + trailing * sine_part,
            trailing * cosine_part - leading * sine_part,
        ],
        axis=-1,
    )


def layer_norm(values, gain, bias):
    centered = values - jnp.mean(values, axis=-1, keepdims=True)
    inverse = lax.rsqrt(jnp.mean(centered * centered, axis=-1, keepdims=True) + NORM_EPSILON)
    normed = centered * inverse
    return (normed * gain + bias, normed, inverse)


def norm_back(incoming, normed, inverse, gain):
    scaled = incoming * gain
    inner = (
        scaled
        - jnp.mean(scaled, axis=-1, keepdims=True)
        - normed * jnp.mean(scaled * normed, axis=-1, keepdims=True)
    )
    return (inner * inverse, jnp.sum(incoming * normed, axis=0), jnp.sum(incoming, axis=0))


def times_transposed(left, right):
    return lax.dot_general(
        left, right, (((1,), (1,)), ((), ())), preferred_element_type=jnp.float32
    )


def transposed_times(left, right):
    return lax.dot_general(
        left, right, (((0,), (0,)), ((), ())), preferred_element_type=jnp.float32
    )


def probabilities(query_rows, key_vectors, query_segments, segments):
    scores = jnp.einsum(
        "qhd,khd->hqk", query_rows, key_vectors, preferred_element_type=jnp.float32
    ) * HD ** (-0.5)
    allowed = (query_segments[:, None] == segments[None, :])[None]
    scores = jnp.where(allowed, scores, -1e30)
    peak = jnp.max(scores, axis=-1, keepdims=True)
    expanded = jnp.where(allowed, jnp.exp(scores - peak), 0.0)
    return expanded / jnp.sum(expanded, axis=-1, keepdims=True)


def attend(queries, key_vectors, value_vectors, segments):
    total_rows = queries.shape[0]
    block_rows = min(512, total_rows)

    def one_block(block_index):
        weights = probabilities(queries, key_vectors, segments, segments)
        return jnp.einsum(
            "hqk,khd->qhd",
            weights.astype(jnp.bfloat16),
            value_vectors,
            preferred_element_type=jnp.float32,
        )

    blocks = lax.map(one_block, jnp.arange(total_rows // block_rows, dtype=jnp.int32))
    return blocks.reshape(queries.shape)


def attend_back(queries, key_vectors, value_vectors, segments, heads_grad):
    total_rows = queries.shape[0]
    block_rows = min(512, total_rows)
    score_scale = HD ** (-0.5)

    def one_block(carry, block_index):
        key_grad, value_grad = carry
        weights = probabilities(queries, key_vectors, segments, segments)
        value_grad = value_grad + jnp.einsum(
            "hqk,qhd->khd",
            weights.astype(jnp.bfloat16),
            heads_grad,
            preferred_element_type=jnp.float32,
        )
        weight_grad = jnp.einsum(
            "qhd,khd->hqk", heads_grad, value_vectors, preferred_element_type=jnp.float32
        )
        centre = jnp.sum(weights * weight_grad, axis=-1, keepdims=True)
        score_grad = (weights * (weight_grad - centre)).astype(jnp.bfloat16)
        query_grad = (
            jnp.einsum("hqk,khd->qhd", score_grad, key_vectors, preferred_element_type=jnp.float32)
            * score_scale
        )
        key_grad = (
            key_grad
            + jnp.einsum("hqk,qhd->khd", score_grad, queries, preferred_element_type=jnp.float32)
            * score_scale
        )
        return ((key_grad, value_grad), query_grad)

    zeros = jnp.zeros(key_vectors.shape, jnp.float32)
    (key_grad, value_grad), query_blocks = lax.scan(
        one_block, (zeros, zeros), jnp.arange(total_rows // block_rows, dtype=jnp.int32)
    )
    return (query_blocks.reshape(queries.shape), key_grad, value_grad)


def join_rows(values):
    return lax.all_gather(values, "mp", axis=0, tiled=True)


def spread_rows(term, part_rows):
    return lax.psum_scatter(
        term(jnp.int32(0), part_rows * lax.axis_size("mp")).astype(jnp.bfloat16),
        "mp",
        scatter_dimension=0,
        tiled=True,
    ).astype(jnp.float32)


def join_grads(values):
    return lax.all_gather(values, "mp", axis=0, tiled=True)


def spread_grads(term, part_rows):
    return lax.psum_scatter(
        term(jnp.int32(0), part_rows * lax.axis_size("mp")).astype(jnp.bfloat16),
        "mp",
        scatter_dimension=0,
        tiled=True,
    ).astype(jnp.float32)


def schulz_step(current, gram):
    mixing = SCHULZ_CUBIC * gram.astype(jnp.float32) + SCHULZ_QUINTIC * jnp.dot(
        gram, gram, preferred_element_type=jnp.float32
    )
    return (
        SCHULZ_LINEAR * current.astype(jnp.float32)
        + jnp.dot(current, mixing.astype(jnp.bfloat16), preferred_element_type=jnp.float32)
    ).astype(jnp.bfloat16)


def gram_part(current):
    return transposed_times(current, current)


def own_piece(whole, place, reference_shape, dp_index, model_width):
    if place == 0:
        qkv_rows = reference_shape[1]
        return lax.dynamic_slice_in_dim(
            whole.reshape(3, -1, model_width), dp_index * qkv_rows, qkv_rows, 1
        )
    shard_rows = reference_shape[0]
    return lax.dynamic_slice_in_dim(whole, dp_index * shard_rows, shard_rows, 0)


def on_device(
    layer_input,
    upstream_grad,
    doc_lengths,
    qkv_weight,
    out_weight,
    gate_weight,
    up_weight,
    down_weight,
    qkv_momentum,
    out_momentum,
    gate_momentum,
    up_momentum,
    down_momentum,
    norm_gains,
    norm_biases,
    adam_first,
    adam_second,
):
    part_rows = layer_input.shape[0]
    model_width = layer_input.shape[1]
    pair_index = lax.axis_index("mp")
    total_rows = part_rows * lax.axis_size("mp")
    shard_list = (
        qkv_weight.astype(jnp.bfloat16),
        out_weight.astype(jnp.bfloat16),
        gate_weight.astype(jnp.bfloat16),
        up_weight.astype(jnp.bfloat16),
        down_weight.astype(jnp.bfloat16),
    )
    fetched = (
        lax.all_gather(shard_list[0], "dp", axis=1, tiled=True),
        lax.all_gather(shard_list[1], "dp", axis=0, tiled=True),
        lax.all_gather(shard_list[2], "dp", axis=0, tiled=True),
        lax.all_gather(shard_list[3], "dp", axis=0, tiled=True),
        lax.all_gather(shard_list[4], "dp", axis=0, tiled=True),
        lax.all_gather(norm_gains.astype(jnp.bfloat16), "dp", axis=1, tiled=True),
        lax.all_gather(norm_biases.astype(jnp.bfloat16), "dp", axis=1, tiled=True),
    )
    qkv_full, out_full, gate_full, up_full, down_full, gains_full, biases_full = fetched
    gains_wide = gains_full.astype(jnp.float32)
    biases_wide = biases_full.astype(jnp.float32)
    local_width = qkv_full.shape[1]
    local_heads = local_width // HD
    segments, positions, validity = document_layout(doc_lengths[0], total_rows)
    cosine_table, sine_table = rotary_tables(positions)
    tokens = join_rows(layer_input)
    projected = times_transposed(tokens, qkv_full.reshape(3 * local_width, model_width))
    columns_split = projected.reshape(total_rows, 3, local_heads, HD)
    queries = rotate(columns_split[:, 0], cosine_table, sine_table).astype(jnp.bfloat16)
    key_vectors = rotate(columns_split[:, 1], cosine_table, sine_table).astype(jnp.bfloat16)
    value_vectors = columns_split[:, 2].astype(jnp.bfloat16)
    attended = attend(queries, key_vectors, value_vectors, segments)
    mixed_heads = attended.reshape(total_rows, local_width).astype(jnp.bfloat16)

    def out_term(offset, span):
        return jnp.dot(mixed_heads, out_full, preferred_element_type=jnp.float32)

    branch = spread_rows(out_term, part_rows)
    first_out, normed_one, inverse_one = layer_norm(
        layer_input.astype(jnp.float32) + branch, gains_wide[0], biases_wide[0]
    )
    inner_rows = first_out.astype(jnp.bfloat16)
    inner_tokens = join_rows(inner_rows)
    gate_pre = times_transposed(inner_tokens, gate_full)
    up_pre = times_transposed(inner_tokens, up_full)
    gate_sigmoid = jax.nn.sigmoid(gate_pre)
    silu_value = gate_pre * gate_sigmoid
    activated = (silu_value * up_pre).astype(jnp.bfloat16)

    def down_term(offset, span):
        return jnp.dot(activated, down_full, preferred_element_type=jnp.float32)

    feed = spread_rows(down_term, part_rows)
    final_out, normed_two, inverse_two = layer_norm(first_out + feed, gains_wide[1], biases_wide[1])
    mixed = final_out.astype(jnp.bfloat16)
    renewed = (
        lax.all_gather(shard_list[0], "dp", axis=1, tiled=True),
        lax.all_gather(shard_list[1], "dp", axis=0, tiled=True),
        lax.all_gather(shard_list[2], "dp", axis=0, tiled=True),
        lax.all_gather(shard_list[3], "dp", axis=0, tiled=True),
        lax.all_gather(shard_list[4], "dp", axis=0, tiled=True),
    )
    qkv_back, out_back, gate_back, up_back, down_back = renewed
    row_valid = lax.dynamic_slice_in_dim(validity, pair_index * part_rows, part_rows, 0)
    cotangent = upstream_grad.astype(jnp.float32) * row_valid[:, None]
    grad_second, gain_two_grad, bias_two_grad = norm_back(
        cotangent, normed_two, inverse_two, gains_wide[1]
    )
    feed_grad = join_grads(grad_second.astype(jnp.bfloat16))
    down_weight_grad = transposed_times(activated, feed_grad)
    hidden_grad = times_transposed(feed_grad, down_back)
    up_grad_rows = (hidden_grad * silu_value).astype(jnp.bfloat16)
    gate_grad_rows = (
        hidden_grad * up_pre * gate_sigmoid * (1.0 + gate_pre * (1.0 - gate_sigmoid))
    ).astype(jnp.bfloat16)
    gate_weight_grad = transposed_times(gate_grad_rows, inner_tokens)
    up_weight_grad = transposed_times(up_grad_rows, inner_tokens)

    def inner_term(offset, span):
        gate_part = jnp.dot(gate_grad_rows, gate_back, preferred_element_type=jnp.float32)
        return gate_part + jnp.dot(up_grad_rows, up_back, preferred_element_type=jnp.float32)

    first_grad_total = grad_second + spread_grads(inner_term, part_rows)
    grad_first, gain_one_grad, bias_one_grad = norm_back(
        first_grad_total, normed_one, inverse_one, gains_wide[0]
    )
    branch_grad = join_grads(grad_first.astype(jnp.bfloat16))
    out_weight_grad = transposed_times(mixed_heads, branch_grad)
    heads_grad = (
        times_transposed(branch_grad, out_back)
        .astype(jnp.bfloat16)
        .reshape(total_rows, local_heads, HD)
    )
    query_grad, key_grad, value_grad = attend_back(
        queries, key_vectors, value_vectors, segments, heads_grad
    )
    stacked_grad = jnp.stack(
        [
            unrotate(query_grad, cosine_table, sine_table),
            unrotate(key_grad, cosine_table, sine_table),
            value_grad,
        ],
        axis=1,
    )
    qkv_grad = stacked_grad.reshape(total_rows, 3 * local_width).astype(jnp.bfloat16)
    qkv_weight_grad = transposed_times(qkv_grad, tokens).reshape(3, local_width, model_width)
    qkv_flat = qkv_back.reshape(3 * local_width, model_width)

    def token_term(offset, span):
        return jnp.dot(qkv_grad, qkv_flat, preferred_element_type=jnp.float32)

    input_grad = grad_first + spread_grads(token_term, part_rows)
    summed = (
        sum_at_owner(qkv_weight_grad.astype(jnp.bfloat16), "dp", 1),
        sum_at_owner(out_weight_grad.astype(jnp.bfloat16), "dp", 0),
        *in_one_piece(
            (
                gate_weight_grad.astype(jnp.bfloat16),
                up_weight_grad.astype(jnp.bfloat16),
                down_weight_grad.astype(jnp.bfloat16),
            ),
            "dp",
            0,
            1,
        ),
    )
    momenta = (qkv_momentum, out_momentum, gate_momentum, up_momentum, down_momentum)
    carried = [MOMENTUM_KEEP * moment + gradient for moment, gradient in zip(momenta, summed)]
    rounded_moments = [value.astype(jnp.bfloat16) for value in carried]
    own_rows = [rounded_moments[0].reshape(-1, model_width)] + rounded_moments[1:]
    square_parts = jnp.stack([jnp.sum(jnp.square(value.astype(jnp.float32))) for value in own_rows])
    norm_grads = jnp.stack([gain_one_grad, gain_two_grad, bias_one_grad, bias_two_grad])
    norm_totals, square_totals = lax.psum((norm_grads, square_parts), ("dp", "mp"))
    dp_index = lax.axis_index("dp")
    gathered = (
        lax.all_gather(rounded_moments[0], "dp", axis=1, tiled=True),
        lax.all_gather(rounded_moments[1], "dp", axis=0, tiled=True),
        lax.all_gather(rounded_moments[2], "dp", axis=0, tiled=True),
        lax.all_gather(rounded_moments[3], "dp", axis=0, tiled=True),
        lax.all_gather(rounded_moments[4], "dp", axis=0, tiled=True),
    )
    matrices = [gathered[0].reshape(-1, model_width)] + list(gathered[1:])
    current = [
        (matrix.astype(jnp.float32) / (jnp.sqrt(square_totals[place]) + 1e-07)).astype(jnp.bfloat16)
        for place, matrix in enumerate(matrices)
    ]
    for repeat in range(ORTHO_STEPS):
        partial_value = [gram_part(matrix) for matrix in current]
        shares = (
            lax.psum_scatter(
                partial_value[0].astype(jnp.bfloat16), "mp", scatter_dimension=0, tiled=True
            ).astype(jnp.float32),
            lax.psum_scatter(
                partial_value[1].astype(jnp.bfloat16), "mp", scatter_dimension=0, tiled=True
            ).astype(jnp.float32),
            lax.psum_scatter(
                partial_value[2].astype(jnp.bfloat16), "mp", scatter_dimension=0, tiled=True
            ).astype(jnp.float32),
            lax.psum_scatter(
                partial_value[3].astype(jnp.bfloat16), "mp", scatter_dimension=0, tiled=True
            ).astype(jnp.float32),
            lax.psum_scatter(
                partial_value[4].astype(jnp.bfloat16), "mp", scatter_dimension=0, tiled=True
            ).astype(jnp.float32),
        )
        shares = [share.astype(jnp.bfloat16) for share in shares]
        grams = (
            lax.all_gather(shares[0], "mp", axis=0, tiled=True),
            lax.all_gather(shares[1], "mp", axis=0, tiled=True),
            lax.all_gather(shares[2], "mp", axis=0, tiled=True),
            lax.all_gather(shares[3], "mp", axis=0, tiled=True),
            lax.all_gather(shares[4], "mp", axis=0, tiled=True),
        )
        current = [schulz_step(matrix, gram) for matrix, gram in zip(current, grams)]
    pieces = [
        own_piece(current[place], place, momenta[place].shape, dp_index, model_width)
        for place in range(5)
    ]
    weights = (qkv_weight, out_weight, gate_weight, up_weight, down_weight)
    row_totals = (3 * D, D, FF, FF, FF)
    updated = [
        weight * (1.0 - ORTHO_RATE * WEIGHT_DECAY)
        - ORTHO_RATE * 0.2 * math.sqrt(row_total) * piece.astype(jnp.float32)
        for weight, piece, row_total in zip(weights, pieces, row_totals)
    ]
    width_part = adam_first.shape[1]
    norm_grad = lax.dynamic_slice_in_dim(norm_totals, dp_index * width_part, width_part, 1)
    norm_now = jnp.concatenate([norm_gains, norm_biases], axis=0)
    norm_first = BETA_FIRST * adam_first + (1.0 - BETA_FIRST) * norm_grad
    norm_second = BETA_SECOND * adam_second + (1.0 - BETA_SECOND) * norm_grad * norm_grad
    first_hat = norm_first / (1.0 - BETA_FIRST**STEP_COUNT)
    second_hat = norm_second / (1.0 - BETA_SECOND**STEP_COUNT)
    norm_updated = norm_now - ADAM_RATE * first_hat / (jnp.sqrt(second_hat) + ADAM_EPSILON)
    return (
        mixed,
        input_grad,
        updated[0],
        updated[1],
        updated[2],
        updated[3],
        updated[4],
        carried[0],
        carried[1],
        carried[2],
        carried[3],
        carried[4],
        norm_updated,
        norm_first,
        norm_second,
    )


def solution(mesh):
    return jax.shard_map(
        on_device,
        mesh=mesh,
        in_specs=(
            P(("dp", "mp"), None),
            P(("dp", "mp"), None),
            P("dp", None),
            P(None, ("mp", "dp"), None),
            P(("mp", "dp"), None),
            P(("mp", "dp"), None),
            P(("mp", "dp"), None),
            P(("mp", "dp"), None),
            P(None, ("mp", "dp"), None),
            P(("mp", "dp"), None),
            P(("mp", "dp"), None),
            P(("mp", "dp"), None),
            P(("mp", "dp"), None),
            P(None, "dp"),
            P(None, "dp"),
            P(None, "dp"),
            P(None, "dp"),
        ),
        out_specs=(
            P(("dp", "mp"), None),
            P(("dp", "mp"), None),
            P(None, ("mp", "dp"), None),
            P(("mp", "dp"), None),
            P(("mp", "dp"), None),
            P(("mp", "dp"), None),
            P(("mp", "dp"), None),
            P(None, ("mp", "dp"), None),
            P(("mp", "dp"), None),
            P(("mp", "dp"), None),
            P(("mp", "dp"), None),
            P(("mp", "dp"), None),
            P(None, "dp"),
            P(None, "dp"),
            P(None, "dp"),
        ),
        check_vma=False,
    )
```

profile of v0, /device:TPU:0, one launch (start us, length us, event | category | flops | bytes accessed | tf_op | source)
XLA Modules:
  0.0 1411.1 jit_solution(11466727412938467774)
XLA Ops:
  19.0 47.1 %all_gather.130 = bf16[384,768]{1,0:T(8,128)(2,1)S(1)} all-gather(bf16[24,768]{1,0:T(8,128)(2,1)S(1)} %convert_element_type.674), channel_id=1, replica_groups=mesh['dp'=16,'mp'=2] {'dp'}, dimensions={0}, use_global_device_ids=true | all-gather | bytes 626688 | tf_op jit(solution)/shard_map/all_gather | solution.py:276
  93.3 38.2 %all-gather = bf16[16,48,2]{1,2,0:T(2,128)(2,1)S(1)} all-gather(bf16[1,48,2]{1,2,0:T(2,128)(2,1)S(1)} %convert_bitcast_fusion.1), channel_id=1, replica_groups=mesh['dp'=16,'mp'=2] {'dp'}, dimensions={0}, use_global_device_ids=true | all-gather | bytes 3264 | tf_op jit(solution)/shard_map/all_gather | solution.py:280
  131.6 35.3 %all-gather.1 = bf16[16,48,2]{1,2,0:T(2,128)(2,1)S(1)} all-gather(bf16[1,48,2]{1,2,0:T(2,128)(2,1)S(1)} %convert_bitcast_fusion), channel_id=1, replica_groups=mesh['dp'=16,'mp'=2] {'dp'}, dimensions={0}, use_global_device_ids=true | all-gather | bytes 3264 | tf_op jit(solution)/shard_map/all_gather | solution.py:281
  178.3 51.9 %all-gather.40.cloned.1.call-done = bf16[1536,768]{1,0:T(8,128)(2,1)} async-done(((bf16[96,768]{1,0:T(8,128)(2,1)}), bf16[1536,768]{1,0:T(8,128)(2,1)}) %all-gather.40.cloned.1.call-update) | async-done | bytes 2359312 | tf_op jit(solution)/shard_map/all_gather | solution.py:278
  236.6 58.3 %all-gather.42.cloned.1.call-done = bf16[1536,768]{1,0:T(8,128)(2,1)} async-done(((bf16[96,768]{1,0:T(8,128)(2,1)}), bf16[1536,768]{1,0:T(8,128)(2,1)}) %all-gather.42.cloned.1.call-update) | async-done | bytes 2359312 | tf_op jit(solution)/shard_map/all_gather | solution.py:279
  379.5 17.5 %all-to-all-done = bf16[16,3,24,768]{3,2,1,0:T(8,128)(2,1)S(1)} async-done(((bf16[16,3,24,768]{3,2,1,0:T(8,128)(2,1)}), bf16[16,3,24,768]{3,2,1,0:T(8,128)(2,1)S(1)}, u32[]{:S(2)}, u32[]{:S(2)}) %all-to-all-start) | async-done | bytes 1769504 | tf_op jit(solution)/shard_map/all_to_all | solution.py:37
  407.9 136.2 %all-to-all-done.2 = bf16[16,96,2304]{2,1,0:T(8,128)(2,1)} async-done(((bf16[16,96,2304]{2,1,0:T(8,128)(2,1)}), bf16[16,96,2304]{2,1,0:T(8,128)(2,1)}, u32[]{:S(2)}, u32[]{:S(2)}) %all-to-all-start.2) | async-done | bytes 7077920 | tf_op jit(solution)/shard_map/all_to_all | solution.py:37
  552.0 41.1 %all-to-all-start.1 = ((bf16[16,24,768]{2,1,0:T(8,128)(2,1)}), bf16[16,24,768]{2,1,0:T(8,128)(2,1)S(1)}, u32[]{:S(2)}, u32[]{:S(2)}) async-start(bf16[16,24,768]{2,1,0:T(8,128)(2,1)} %bitcast.35), calls=%async_computation.5 | async-start | bytes 1179648 | tf_op jit(solution)/shard_map/all_to_all | solution.py:37
  593.2 17.6 %all-to-all-done.1 = bf16[16,24,768]{2,1,0:T(8,128)(2,1)S(1)} async-done(((bf16[16,24,768]{2,1,0:T(8,128)(2,1)}), bf16[16,24,768]{2,1,0:T(8,128)(2,1)S(1)}, u32[]{:S(2)}, u32[]{:S(2)}) %all-to-all-start.1) | async-done | bytes 589856 | tf_op jit(solution)/shard_map/all_to_all | solution.py:37
  615.5 43.7 %all_gather.145 = bf16[384,768]{1,0:T(8,128)(2,1)S(1)} all-gather(bf16[24,768]{1,0:T(8,128)(2,1)S(1)} %get-tuple-element.87), channel_id=1, replica_groups=mesh['dp'=16,'mp'=2] {'dp'}, dimensions={0}, use_global_device_ids=true | all-gather | bytes 626688 | tf_op jit(solution)/shard_map/all_gather | solution.py:401
  659.2 38.1 %all-reduce = (f32[5]{0:T(128)S(1)}, f32[4,768]{1,0:T(4,128)}) all-reduce(f32[5]{0:T(128)S(1)} %stack.54, f32[4,768]{1,0:T(4,128)S(1)} %pad_maximum_fusion.15), channel_id=1, replica_groups=mesh['dp'=16,'mp'=2] {'dp','mp'}, use_global_device_ids=true, to_apply=%region_26.27 | all-reduce | flops 3077 | bytes 24616 | tf_op jit(solution)/shard_map/psum | solution.py:397
  730.0 11.9 reduce-scatter.38.cloned.1.call-done
  742.6 66.5 %all-gather.90.cloned.1.call-done = bf16[1536,768]{1,0:T(8,128)(2,1)} async-done(((bf16[96,768]{1,0:T(8,128)(2,1)}), bf16[1536,768]{1,0:T(8,128)(2,1)}) %all-gather.90.cloned.1.call-update) | async-done | bytes 2359312 | tf_op jit(solution)/shard_map/all_gather | solution.py:404
  818.9 11.9 reduce-scatter.68.cloned.1.call-done
  830.9 11.8 all-gather.56.cloned.1.call-done
  866.7 11.9 all-gather.68.cloned.1.call-done
  914.9 11.9 all-gather.92.cloned.1.call-done
  951.1 11.8 all-gather.58.cloned.1.call-done
  986.8 12.0 all-gather.70.cloned.1.call-done
  1035.1 11.8 all-gather.94.cloned.1.call-done
  1059.9 11.5 reduce-scatter.72.cloned.1.call-done
  1071.4 11.8 all-gather.60.cloned.1.call-done
  1107.4 11.8 all-gather.72.cloned.1.call-done
  1143.3 12.2 reduce-scatter.44.cloned.1.call-done
  1155.5 11.8 all-gather.96.cloned.1.call-done
  1179.5 12.0 reduce-scatter.74.cloned.1.call-done
  1191.6 11.8 all-gather.62.cloned.1.call-done
  1227.2 11.9 all-gather.74.cloned.1.call-done
  1275.3 11.8 all-gather.98.cloned.1.call-done
  1299.5 11.6 reduce-scatter.36.cloned.1.call-done
  1323.6 11.7 all-gather.64.cloned.1.call-done
  1359.1 12.0 all-gather.76.cloned.1.call-done
  (458 shorter events, 562.9 us)
Async XLA Ops:
  8.8 158.3 %reduce-scatter.30.cloned.1.call-start = ((), (), s32[]{:S(2)}) async-start(), calls=%async_computation.33 | async-start | bytes 1179648 | tf_op jit(solution)/shard_map/reduce_scatter | solution.py:199
  90.9 82.3 %all-gather.38.cloned.1.call-start = ((), (), s32[]{:S(2)}) async-start(), calls=%async_computation.34 | async-start | bytes 2506752 | tf_op jit(solution)/shard_map/all_gather | solution.py:277
  91.7 138.5 %all-gather.40.cloned.1.call-start = ((), (), s32[]{:S(2)}) async-start(), calls=%async_computation.35 | async-start | bytes 2506752 | tf_op jit(solution)/shard_map/all_gather | solution.py:278
  92.4 202.5 %all-gather.42.cloned.1.call-start = ((), (), s32[]{:S(2)}) async-start(), calls=%async_computation.36 | async-start | bytes 2506752 | tf_op jit(solution)/shard_map/all_gather | solution.py:279
  93.2 213.4 %reduce-scatter.32.cloned.1.call-start = ((), (), s32[]{:S(2)}) async-start(), calls=%async_computation.37 | async-start | bytes 1179648 | tf_op jit(solution)/shard_map/reduce_scatter | solution.py:199
  396.9 147.3 %all-to-all-start.2 = ((bf16[16,96,2304]{2,1,0:T(8,128)(2,1)}), bf16[16,96,2304]{2,1,0:T(8,128)(2,1)}, u32[]{:S(2)}, u32[]{:S(2)}) async-start(bf16[16,96,2304]{2,1,0:T(8,128)(2,1)} %bitcast.229), calls=%async_computation.6 | async-start | bytes 14155776 | tf_op jit(solution)/shard_map/all_to_all | solution.py:37
  406.2 295.0 %all-gather.44.cloned.1.call-start = ((), (), s32[]{:S(2)}) async-start(), calls=%async_computation.40 | async-start | bytes 1880064 | tf_op jit(solution)/shard_map/all_gather | solution.py:400
  407.9 300.0 %all-gather.66.cloned.1.call-start = ((), (), s32[]{:S(2)}) async-start(), calls=%async_computation.61 | async-start | bytes 2506752 | tf_op jit(solution)/shard_map/all_gather | solution.py:402
  550.1 169.9 %all-gather.78.cloned.1.call-start = ((), (), s32[]{:S(2)}) async-start(), calls=%async_computation.72 | async-start | bytes 2506752 | tf_op jit(solution)/shard_map/all_gather | solution.py:403
  593.1 136.8 %reduce-scatter.48.cloned.1.call-start = ((), (), s32[]{:S(2)}) async-start(), calls=%async_computation.51 | async-start | bytes 1769472 | tf_op jit(solution)/shard_map/reduce_scatter | solution.py:417
  706.0 103.1 %all-gather.90.cloned.1.call-start = ((), (), s32[]{:S(2)}) async-start(), calls=%async_computation.83 | async-start | bytes 2506752 | tf_op jit(solution)/shard_map/all_gather | solution.py:404
  706.8 112.1 %reduce-scatter.58.cloned.1.call-start = ((), (), s32[]{:S(2)}) async-start(), calls=%async_computation.62 | async-start | bytes 1769472 | tf_op jit(solution)/shard_map/reduce_scatter | solution.py:420
  713.5 117.4 %reduce-scatter.68.cloned.1.call-start = ((), (), s32[]{:S(2)}) async-start(), calls=%async_computation.73 | async-start | bytes 1769472 | tf_op jit(solution)/shard_map/reduce_scatter | solution.py:423
  725.6 117.1 %all-gather.56.cloned.1.call-start = ((), (), s32[]{:S(2)}) async-start(), calls=%async_computation.52 | async-start | bytes 1769472 | tf_op jit(solution)/shard_map/all_gather | solution.py:433
  729.9 124.7 %all-gather.46.cloned.1.call-start = ((), (), s32[]{:S(2)}) async-start(), calls=%async_computation.42 | async-start | bytes 1769472 | tf_op jit(solution)/shard_map/all_gather | solution.py:432
  741.9 124.8 %reduce-scatter.78.cloned.1.call-start = ((), (), s32[]{:S(2)}) async-start(), calls=%async_computation.84 | async-start | bytes 1769472 | tf_op jit(solution)/shard_map/reduce_scatter | solution.py:426
  818.9 72.8 %all-gather.80.cloned.1.call-start = ((), (), s32[]{:S(2)}) async-start(), calls=%async_computation.74 | async-start | bytes 1769472 | tf_op jit(solution)/shard_map/all_gather | solution.py:435
  830.8 73.6 %reduce-scatter.50.cloned.1.call-start = ((), (), s32[]{:S(2)}) async-start(), calls=%async_computation.53 | async-start | bytes 1769472 | tf_op jit(solution)/shard_map/reduce_scatter | solution.py:417
  866.7 72.5 %reduce-scatter.60.cloned.1.call-start = ((), (), s32[]{:S(2)}) async-start(), calls=%async_computation.64 | async-start | bytes 1769472 | tf_op jit(solution)/shard_map/reduce_scatter | solution.py:420
  914.8 71.9 %reduce-scatter.80.cloned.1.call-start = ((), (), s32[]{:S(2)}) async-start(), calls=%async_computation.86 | async-start | bytes 1769472 | tf_op jit(solution)/shard_map/reduce_scatter | solution.py:426
  951.0 73.1 %reduce-scatter.52.cloned.1.call-start = ((), (), s32[]{:S(2)}) async-start(), calls=%async_computation.55 | async-start | bytes 1769472 | tf_op jit(solution)/shard_map/reduce_scatter | solution.py:417
  986.8 72.5 %reduce-scatter.62.cloned.1.call-start = ((), (), s32[]{:S(2)}) async-start(), calls=%async_computation.66 | async-start | bytes 1769472 | tf_op jit(solution)/shard_map/reduce_scatter | solution.py:420
  1035.1 72.2 %reduce-scatter.82.cloned.1.call-start = ((), (), s32[]{:S(2)}) async-start(), calls=%async_computation.88 | async-start | bytes 1769472 | tf_op jit(solution)/shard_map/reduce_scatter | solution.py:426
  1059.8 72.0 %all-gather.84.cloned.1.call-start = ((), (), s32[]{:S(2)}) async-start(), calls=%async_computation.78 | async-start | bytes 1769472 | tf_op jit(solution)/shard_map/all_gather | solution.py:435
  1107.3 72.1 %reduce-scatter.64.cloned.1.call-start = ((), (), s32[]{:S(2)}) async-start(), calls=%async_computation.68 | async-start | bytes 1769472 | tf_op jit(solution)/shard_map/reduce_scatter | solution.py:420
  1179.4 74.5 %all-gather.86.cloned.1.call-start = ((), (), s32[]{:S(2)}) async-start(), calls=%async_computation.80 | async-start | bytes 1769472 | tf_op jit(solution)/shard_map/all_gather | solution.py:435
  1191.5 72.1 %reduce-scatter.56.cloned.1.call-start = ((), (), s32[]{:S(2)}) async-start(), calls=%async_computation.59 | async-start | bytes 1769472 | tf_op jit(solution)/shard_map/reduce_scatter | solution.py:417
  1227.1 72.2 %reduce-scatter.66.cloned.1.call-start = ((), (), s32[]{:S(2)}) async-start(), calls=%async_computation.70 | async-start | bytes 1769472 | tf_op jit(solution)/shard_map/reduce_scatter | solution.py:420
  1264.3 82.8 %all-gather.54.cloned.1.call-start = ((), (), s32[]{:S(2)}) async-start(), calls=%async_computation.50 | async-start | bytes 1769472 | tf_op jit(solution)/shard_map/all_gather | solution.py:432
  1275.3 83.8 %reduce-scatter.86.cloned.1.call-start = ((), (), s32[]{:S(2)}) async-start(), calls=%async_computation.92 | async-start | bytes 1769472 | tf_op jit(solution)/shard_map/reduce_scatter | solution.py:426
  1296.9 74.3 %all-gather.76.cloned.1.call-start = ((), (), s32[]{:S(2)}) async-start(), calls=%async_computation.71 | async-start | bytes 1769472 | tf_op jit(solution)/shard_map/all_gather | solution.py:434
  1299.4 83.8 %all-gather.88.cloned.1.call-start = ((), (), s32[]{:S(2)}) async-start(), calls=%async_computation.82 | async-start | bytes 1769472 | tf_op jit(solution)/shard_map/all_gather | solution.py:435
  (106 other events, 3279.5 us)
Sparse Core Ops, SparseCore 0:
  11.3 63.0 all-gather.35
  101.8 63.5 all-gather.37
  169.0 61.0 all-gather.39
  233.8 61.0 all-gather.41
  410.6 150.8 all-gather.43
  565.3 88.6 all-gather.65
  657.6 62.4 all-gather.77
  745.6 63.4 all-gather.89
  832.3 10.4 all-gather.55
  844.2 10.3 all-gather.45
  868.2 10.4 all-gather.67
  880.1 10.3 all-gather.79
  916.4 10.4 all-gather.91
  952.4 10.4 all-gather.57
  964.2 10.3 all-gather.47
  988.4 10.4 all-gather.69
  1000.3 10.3 all-gather.81
  1036.5 10.4 all-gather.93
  1072.8 10.4 all-gather.59
  1084.7 10.3 all-gather.49
  1108.7 10.4 all-gather.71
  1120.7 10.3 all-gather.83
  1156.9 10.4 all-gather.95
  1192.9 10.4 all-gather.61
  1204.7 10.3 all-gather.51
  1228.6 10.4 all-gather.73
  1240.7 10.3 all-gather.85
  1276.7 10.4 all-gather.97
  1324.8 10.4 all-gather.63
  1336.7 10.3 all-gather.53
  1360.7 10.4 all-gather.75
  1372.8 10.3 all-gather.87
  (30 shorter events, 282.6 us)
where the time goes:
time: 1420 us; the launch traced here: 1410 us
  waiting for transfers between devices  729 us (51%)
  matrix products  317 us (22%)
  blocking collectives  214 us (15%)
  starting transfers between devices  62.4 us (4%)
  other arithmetic  48.5 us (3%)
  local copies, waits for them, and re-layouts  20.5 us (1%)
  between operations  19.7 us (1%)
    all_to_all x3, waiting for transfers between devices, sum_at_owner(): lax.all_to_all(pieces, axis, split_axis=0, concat_axis=0, tiled=True)  171 us
    dot_general x25, matrix products, schulz_step(): jnp.dot(current, mixing.astype(jnp.bfloat16), preferred_element_type=jnp....  152 us
    dot_general x30, matrix products, transposed_times(): lax.dot_general(left, right, (((0,), (0,)), ((), ())), preferred_element_...  115 us
    all_gather x1, waiting for transfers between devices, on_device(): lax.all_gather(rounded_moments[4], 'dp', axis=0, tiled=True)  66.5 us
    all_gather x5, waiting for transfers between devices, on_device(): lax.all_gather(shares[2], 'mp', axis=0, tiled=True)  59.6 us
    all_gather x5, waiting for transfers between devices, on_device(): lax.all_gather(shares[1], 'mp', axis=0, tiled=True)  58.9 us
    all_gather x1, waiting for transfers between devices, on_device(): lax.all_gather(shard_list[4], 'dp', axis=0, tiled=True)  58.3 us
    all_to_all x3, starting transfers between devices, sum_at_owner(): lax.all_to_all(pieces, axis, split_axis=0, concat_axis=0, tiled=True)  57.3 us
  transfers between devices with their start and end apart: 65, of which 52 were waited for; matrix products, arithmetic and copies ran while one was open for 23% of the time, Pallas kernels for 0%

commit v1 on v0

v1 whole, which is shorter than its diff:
```python
import math

import jax
import jax.numpy as jnp
from jax import lax
from jax.sharding import PartitionSpec as P

D = 768
HD = 64
FF = 3072
ORTHO_STEPS = 5
STEP_COUNT = 10


NORM_EPSILON = 1e-12
ROPE_BASE = 1000.0
SCHULZ_LINEAR = 3.4445
SCHULZ_CUBIC = -4.775
SCHULZ_QUINTIC = 2.0315
MOMENTUM_KEEP = 0.5
ORTHO_RATE = 0.2
WEIGHT_DECAY = 0.01
ADAM_RATE = 0.2
BETA_FIRST = 0.9
BETA_SECOND = 0.95
ADAM_EPSILON = 1e-08


def rotary_tables(positions):
    half_width = HD // 2
    exponents = jnp.arange(half_width, dtype=jnp.float32) * (2.0 / HD)
    frequency = jnp.power(jnp.float32(ROPE_BASE), -exponents)
    angles = positions.astype(jnp.float32)[:, None] * frequency[None, :]
    return (jnp.cos(angles), jnp.sin(angles))


def rotate(vectors, cosine_table, sine_table):
    half_width = vectors.shape[-1] // 2
    leading = vectors[..., :half_width]
    trailing = vectors[..., half_width:]
    cosine_part = cosine_table[:, None, :]
    sine_part = sine_table[:, None, :]
    return jnp.concatenate(
        [
            leading * cosine_part - trailing * sine_part,
            trailing * cosine_part + leading * sine_part,
        ],
        axis=-1,
    )


def unrotate(gradients, cosine_table, sine_table):
    half_width = gradients.shape[-1] // 2
    leading = gradients[..., :half_width]
    trailing = gradients[..., half_width:]
    cosine_part = cosine_table[:, None, :]
    sine_part = sine_table[:, None, :]
    return jnp.concatenate(
        [
            leading * cosine_part + trailing * sine_part,
            trailing * cosine_part - leading * sine_part,
        ],
        axis=-1,
    )


def layer_norm(values, gain, bias):
    centered = values - jnp.mean(values, axis=-1, keepdims=True)
    inverse = lax.rsqrt(jnp.mean(centered * centered, axis=-1, keepdims=True) + NORM_EPSILON)
    normed = centered * inverse
    return (normed * gain + bias, normed, inverse)


def norm_back(incoming, normed, inverse, gain):
    scaled = incoming * gain
    inner = (
        scaled
        - jnp.mean(scaled, axis=-1, keepdims=True)
        - normed * jnp.mean(scaled * normed, axis=-1, keepdims=True)
    )
    return (inner * inverse, jnp.sum(incoming * normed, axis=0), jnp.sum(incoming, axis=0))


def times_transposed(left, right):
    return lax.dot_general(
        left, right, (((1,), (1,)), ((), ())), preferred_element_type=jnp.float32
    )


def transposed_times(left, right):
    return lax.dot_general(
        left, right, (((0,), (0,)), ((), ())), preferred_element_type=jnp.float32
    )


def probabilities(query_rows, key_vectors, query_segments, segments):
    scores = jnp.einsum(
        "qhd,khd->hqk", query_rows, key_vectors, preferred_element_type=jnp.float32
    ) * HD ** (-0.5)
    allowed = (query_segments[:, None] == segments[None, :])[None]
    scores = jnp.where(allowed, scores, -1e30)
    peak = jnp.max(scores, axis=-1, keepdims=True)
    expanded = jnp.where(allowed, jnp.exp(scores - peak), 0.0)
    return expanded / jnp.sum(expanded, axis=-1, keepdims=True)


def attend(queries, key_vectors, value_vectors, segments):
    total_rows = queries.shape[0]
    block_rows = min(512, total_rows)

    def one_block(block_index):
        weights = probabilities(queries, key_vectors, segments, segments)
        return jnp.einsum(
            "hqk,khd->qhd",
            weights.astype(jnp.bfloat16),
            value_vectors,
            preferred_element_type=jnp.float32,
        )

    blocks = lax.map(one_block, jnp.arange(total_rows // block_rows, dtype=jnp.int32))
    return blocks.reshape(queries.shape)


def attend_back(queries, key_vectors, value_vectors, segments, heads_grad):
    total_rows = queries.shape[0]
    block_rows = min(512, total_rows)
    score_scale = HD ** (-0.5)

    def one_block(carry, block_index):
        key_grad, value_grad = carry
        weights = probabilities(queries, key_vectors, segments, segments)
        value_grad = value_grad + jnp.einsum(
            "hqk,qhd->khd",
            weights.astype(jnp.bfloat16),
            heads_grad,
            preferred_element_type=jnp.float32,
        )
        weight_grad = jnp.einsum(
            "qhd,khd->hqk", heads_grad, value_vectors, preferred_element_type=jnp.float32
        )
        centre = jnp.sum(weights * weight_grad, axis=-1, keepdims=True)
        score_grad = (weights * (weight_grad - centre)).astype(jnp.bfloat16)
        query_grad = (
            jnp.einsum("hqk,khd->qhd", score_grad, key_vectors, preferred_element_type=jnp.float32)
            * score_scale
        )
        key_grad = (
            key_grad
            + jnp.einsum("hqk,qhd->khd", score_grad, queries, preferred_element_type=jnp.float32)
            * score_scale
        )
        return ((key_grad, value_grad), query_grad)

    zeros = jnp.zeros(key_vectors.shape, jnp.float32)
    (key_grad, value_grad), query_blocks = lax.scan(
        one_block, (zeros, zeros), jnp.arange(total_rows // block_rows, dtype=jnp.int32)
    )
    return (query_blocks.reshape(queries.shape), key_grad, value_grad)


def swap(value):
    return lax.ppermute(value, "mp", [(0, 1), (1, 0)])


def flip(value, mask):
    count = lax.axis_size("dp")
    return lax.ppermute(value, "dp", [(i, i ^ mask) for i in range(count)])


def index_bits(count):
    bits = count.bit_length() - 1
    side = (bits - 2) // 2
    return (
        [1 << k for k in range(bits - 2, bits)],
        [1 << k for k in range(side)],
        [1 << k for k in range(side, bits - 2)],
    )


def block_codes(count):
    z_bits, x_bits, y_bits = index_bits(count)
    codes = [0]
    for mask in z_bits + x_bits + y_bits:
        codes = codes + [code ^ mask for code in codes]
    return codes


def lane_split(width):
    return width // 256 * 128


def gather_blocks(shard):
    z_bits, x_bits, y_bits = index_bits(lax.axis_size("dp"))
    low, high = z_bits
    shard = shard[None]
    column = jnp.concatenate(
        [shard, flip(shard, low), flip(shard, high), flip(shard, low ^ high)], axis=0
    )
    if len(x_bits) > 1:
        for mask in x_bits + y_bits:
            column = jnp.concatenate([column, flip(column, mask)], axis=0)
        return column
    x_mask, y_mask = x_bits[0], y_bits[0]
    cut = lane_split(column.shape[-1])
    along_x, along_y = flip(column, x_mask), flip(column, y_mask)
    across = jnp.concatenate(
        [flip(along_y[..., :cut], x_mask), flip(along_x[..., cut:], y_mask)], axis=-1
    )
    return jnp.concatenate([column, along_x, along_y, across], axis=0)


def scatter_blocks(blocks):
    z_bits, x_bits, y_bits = index_bits(lax.axis_size("dp"))

    def sent(value, mask):
        return flip(value.astype(jnp.bfloat16), mask).astype(jnp.float32)

    if len(x_bits) > 1:
        for mask in reversed(x_bits + y_bits):
            half = blocks.shape[0] // 2
            blocks = blocks[:half].astype(jnp.float32) + sent(blocks[half:], mask)
    else:
        x_mask, y_mask = x_bits[0], y_bits[0]
        cut = lane_split(blocks.shape[-1])
        here, along_x, along_y, across = [blocks[4 * k : 4 * k + 4] for k in range(4)]
        by_x = sent(across[..., :cut], x_mask)
        by_y = sent(across[..., cut:], y_mask)
        along_y = jnp.concatenate(
            [along_y[..., :cut].astype(jnp.float32) + by_x, along_y[..., cut:].astype(jnp.float32)],
            axis=-1,
        )
        along_x = jnp.concatenate(
            [along_x[..., :cut].astype(jnp.float32), along_x[..., cut:].astype(jnp.float32) + by_y],
            axis=-1,
        )
        blocks = here.astype(jnp.float32) + sent(along_x, x_mask) + sent(along_y, y_mask)
    low, high = z_bits
    return (
        blocks[0] + sent(blocks[1], low) + sent(blocks[2], high) + sent(blocks[3], low ^ high)
    )


def block_places(count, rows):
    codes = jnp.repeat(jnp.asarray(block_codes(count), jnp.int32), rows)
    offsets = jnp.tile(jnp.arange(rows, dtype=jnp.int32), count)
    return (codes ^ lax.axis_index("dp")) * rows + offsets


def one_hot_rows(places, count):
    return (jnp.arange(count, dtype=jnp.int32)[:, None] == places[None, :]).astype(jnp.bfloat16)


def chosen(rows, order):
    return jnp.dot(rows, order, preferred_element_type=jnp.float32).astype(jnp.bfloat16)


def document_rows(lengths, row_ids):
    ends = jnp.cumsum(lengths)
    starts = ends - lengths
    segments = jnp.sum((row_ids[:, None] >= ends[None, :]).astype(jnp.int32), axis=1)
    used_rows = ends[-1]
    matches = segments[:, None] == jnp.arange(lengths.shape[0], dtype=jnp.int32)[None, :]
    anchor = jnp.sum(jnp.where(matches, starts[None, :], 0), axis=1)
    anchor = anchor + jnp.where(segments == lengths.shape[0], used_rows, 0)
    validity = (row_ids < used_rows).astype(jnp.float32)
    return (segments, row_ids - anchor, validity)


def schulz(gram, rows):
    scale = 1.0 / (jnp.sqrt(jnp.trace(gram.astype(jnp.float32))) + 1e-07)
    gram = gram.astype(jnp.float32) * scale * scale
    current = (rows.astype(jnp.float32) * scale).astype(jnp.bfloat16)
    for repeat in range(ORTHO_STEPS):
        narrow = gram.astype(jnp.bfloat16)
        mixing = (
            SCHULZ_CUBIC * gram
            + SCHULZ_QUINTIC * jnp.dot(narrow, narrow, preferred_element_type=jnp.float32)
        ).astype(jnp.bfloat16)
        current = (
            SCHULZ_LINEAR * current.astype(jnp.float32)
            + jnp.dot(current, mixing, preferred_element_type=jnp.float32)
        ).astype(jnp.bfloat16)
        once = SCHULZ_LINEAR * gram + jnp.dot(narrow, mixing, preferred_element_type=jnp.float32)
        gram = SCHULZ_LINEAR * once + jnp.dot(
            once.astype(jnp.bfloat16), mixing, preferred_element_type=jnp.float32
        )
    return current


def spread(term, own_rows):
    return term[:own_rows] + swap(term[own_rows:].astype(jnp.bfloat16)).astype(jnp.float32)


def join(values):
    return jnp.concatenate([values, swap(values)], axis=0)


def on_device(
    layer_input,
    upstream_grad,
    doc_lengths,
    qkv_weight,
    out_weight,
    gate_weight,
    up_weight,
    down_weight,
    qkv_momentum,
    out_momentum,
    gate_momentum,
    up_momentum,
    down_momentum,
    norm_gains,
    norm_biases,
    adam_first,
    adam_second,
):
    part_rows, model_width = layer_input.shape
    core = lax.axis_index("mp")
    dp_count = lax.axis_size("dp")
    dp_index = lax.axis_index("dp")
    head_rows = out_weight.shape[0]
    hidden_rows = gate_weight.shape[0]
    local_width = head_rows * dp_count
    local_heads = local_width // HD
    local_hidden = hidden_rows * dp_count

    tokens = join(layer_input)
    norm_params = jnp.concatenate([norm_gains, norm_biases])
    norm_width = norm_params.shape[1]
    norm_pad = jnp.pad(norm_params.reshape(1, -1), ((0, 15), (0, model_width - 4 * norm_width)))
    attn_blocks = gather_blocks(
        jnp.concatenate(
            [qkv_weight.reshape(-1, model_width), out_weight, norm_pad], axis=0
        ).astype(jnp.bfloat16)
    )
    gate_up_blocks = gather_blocks(
        jnp.concatenate([gate_weight, up_weight], axis=0).astype(jnp.bfloat16)
    )
    down_blocks = gather_blocks(down_weight.astype(jnp.bfloat16))

    pair_rows = 2 * head_rows
    places = block_places(dp_count, pair_rows)
    kind, place = places % pair_rows // head_rows, places // pair_rows * head_rows
    head_order = one_hot_rows(
        kind * local_width + place + places % head_rows, 2 * local_width
    )
    query_key_weight = chosen(
        head_order, attn_blocks[:, :pair_rows].reshape(2 * local_width, model_width)
    )
    value_out_weight = chosen(
        head_order, attn_blocks[:, pair_rows : 2 * pair_rows].reshape(2 * local_width, model_width)
    )
    qkv_flat = jnp.concatenate([query_key_weight, value_out_weight[:local_width]], axis=0)
    out_full = value_out_weight[local_width:]
    norm_blocks = attn_blocks[:, 2 * pair_rows, : 4 * norm_width].reshape(dp_count, 4, norm_width)
    norm_order = one_hot_rows(block_places(dp_count, 1), dp_count)
    norm_wide = jnp.einsum(
        "ij,jpw->piw", norm_order, norm_blocks, preferred_element_type=jnp.float32
    ).reshape(4, model_width)
    gains_wide, biases_wide = norm_wide[:2], norm_wide[2:]
    gate_full = gate_up_blocks[:, :hidden_rows].reshape(local_hidden, model_width)
    up_full = gate_up_blocks[:, hidden_rows:].reshape(local_hidden, model_width)
    down_full = down_blocks.reshape(local_hidden, model_width)

    own_ids = core * part_rows + jnp.arange(part_rows, dtype=jnp.int32)
    other_ids = (1 - core) * part_rows + jnp.arange(part_rows, dtype=jnp.int32)
    segments, positions, validity = document_rows(
        doc_lengths[0], jnp.concatenate([own_ids, other_ids])
    )
    total_rows = 2 * part_rows
    cosine_table, sine_table = rotary_tables(positions)
    projected = times_transposed(tokens, qkv_flat)
    columns_split = projected.reshape(total_rows, 3, local_heads, HD)
    queries = rotate(columns_split[:, 0], cosine_table, sine_table).astype(jnp.bfloat16)
    key_vectors = rotate(columns_split[:, 1], cosine_table, sine_table).astype(jnp.bfloat16)
    value_vectors = columns_split[:, 2].astype(jnp.bfloat16)
    attended = attend(queries, key_vectors, value_vectors, segments)
    mixed_heads = attended.reshape(total_rows, local_width).astype(jnp.bfloat16)
    branch = spread(jnp.dot(mixed_heads, out_full, preferred_element_type=jnp.float32), part_rows)
    first_out, normed_one, inverse_one = layer_norm(
        layer_input.astype(jnp.float32) + branch, gains_wide[0], biases_wide[0]
    )
    inner_tokens = join(first_out.astype(jnp.bfloat16))
    gate_pre = times_transposed(inner_tokens, gate_full)
    up_pre = times_transposed(inner_tokens, up_full)
    gate_sigmoid = jax.nn.sigmoid(gate_pre)
    silu_value = gate_pre * gate_sigmoid
    activated = (silu_value * up_pre).astype(jnp.bfloat16)
    feed = spread(jnp.dot(activated, down_full, preferred_element_type=jnp.float32), part_rows)
    final_out, normed_two, inverse_two = layer_norm(first_out + feed, gains_wide[1], biases_wide[1])
    mixed = final_out.astype(jnp.bfloat16)

    cotangent = upstream_grad.astype(jnp.float32) * validity[:part_rows, None]
    grad_second, gain_two_grad, bias_two_grad = norm_back(
        cotangent, normed_two, inverse_two, gains_wide[1]
    )
    feed_grad = join(grad_second.astype(jnp.bfloat16))
    down_weight_grad = transposed_times(activated, feed_grad).astype(jnp.bfloat16)
    down_sum = scatter_blocks(down_weight_grad.reshape(dp_count, hidden_rows, model_width))
    hidden_grad = times_transposed(feed_grad, down_full)
    up_grad_rows = (hidden_grad * silu_value).astype(jnp.bfloat16)
    gate_grad_rows = (
        hidden_grad * up_pre * gate_sigmoid * (1.0 + gate_pre * (1.0 - gate_sigmoid))
    ).astype(jnp.bfloat16)
    inner_grad = jnp.dot(gate_grad_rows, gate_full, preferred_element_type=jnp.float32) + jnp.dot(
        up_grad_rows, up_full, preferred_element_type=jnp.float32
    )
    gate_weight_grad = transposed_times(gate_grad_rows, inner_tokens).astype(jnp.bfloat16)
    up_weight_grad = transposed_times(up_grad_rows, inner_tokens).astype(jnp.bfloat16)
    gate_up_sum = scatter_blocks(
        jnp.concatenate(
            [
                gate_weight_grad.reshape(dp_count, hidden_rows, model_width),
                up_weight_grad.reshape(dp_count, hidden_rows, model_width),
            ],
            axis=1,
        )
    )
    first_grad_total = grad_second + spread(inner_grad, part_rows)
    grad_first, gain_one_grad, bias_one_grad = norm_back(
        first_grad_total, normed_one, inverse_one, gains_wide[0]
    )
    branch_grad = join(grad_first.astype(jnp.bfloat16))
    padded_rows = head_rows + -head_rows % 16
    single_order = jnp.pad(
        one_hot_rows(block_places(dp_count, head_rows), local_width).reshape(
            local_width, dp_count, head_rows
        ),
        ((0, 0), (0, 0), (0, padded_rows - head_rows)),
    ).reshape(local_width, dp_count * padded_rows)
    out_weight_grad = transposed_times(chosen(mixed_heads, single_order), branch_grad)
    out_sum = scatter_blocks(
        out_weight_grad.astype(jnp.bfloat16).reshape(dp_count, padded_rows, model_width)
    )[:head_rows]
    heads_grad = (
        times_transposed(branch_grad, out_full)
        .astype(jnp.bfloat16)
        .reshape(total_rows, local_heads, HD)
    )
    query_grad, key_grad, value_grad = attend_back(
        queries, key_vectors, value_vectors, segments, heads_grad
    )
    query_key_grad = jnp.concatenate(
        [
            unrotate(query_grad, cosine_table, sine_table).reshape(total_rows, local_width),
            unrotate(key_grad, cosine_table, sine_table).reshape(total_rows, local_width),
        ],
        axis=1,
    ).astype(jnp.bfloat16)
    value_grad = value_grad.reshape(total_rows, local_width).astype(jnp.bfloat16)
    qkv_grad = jnp.concatenate([query_key_grad, value_grad], axis=1)
    qkv_weight_grad = jnp.concatenate(
        [
            transposed_times(chosen(query_key_grad, head_order), tokens)
            .astype(jnp.bfloat16)
            .reshape(dp_count, pair_rows, model_width),
            transposed_times(chosen(value_grad, single_order), tokens)
            .astype(jnp.bfloat16)
            .reshape(dp_count, padded_rows, model_width),
        ],
        axis=1,
    )
    qkv_sum = scatter_blocks(qkv_weight_grad)[: 3 * head_rows].reshape(qkv_weight.shape)
    input_grad = grad_first + spread(
        jnp.dot(qkv_grad, qkv_flat, preferred_element_type=jnp.float32), part_rows
    )

    norm_totals = jnp.stack([gain_one_grad, gain_two_grad, bias_one_grad, bias_two_grad])
    norm_totals = norm_totals + swap(norm_totals)
    for mask in [1 << k for k in range(dp_count.bit_length() - 1)]:
        norm_totals = norm_totals + flip(norm_totals, mask)

    momenta = (qkv_momentum, out_momentum, gate_momentum, up_momentum, down_momentum)
    summed = (qkv_sum, out_sum, gate_up_sum[:hidden_rows], gate_up_sum[hidden_rows:], down_sum)
    carried = [MOMENTUM_KEEP * moment + gradient for moment, gradient in zip(momenta, summed)]
    qkv_rows, out_rows, gate_rows, up_rows, down_rows = [
        value.astype(jnp.bfloat16).reshape(-1, model_width) for value in carried
    ]

    first_core = core == 0
    lent = swap(jnp.stack([jnp.where(first_core, down_rows, gate_rows), up_rows]))
    pair_one = jnp.concatenate([jnp.where(first_core, gate_rows, down_rows), lent[0]])
    pair_up = jnp.concatenate([up_rows, lent[1]])
    block = model_width // dp_count
    half_width = model_width // 2
    order = one_hot_rows(block_places(dp_count, block), model_width)
    half_up = jnp.where(first_core, pair_up[:, :half_width], pair_up[:, half_width:])
    gram_rows = jnp.concatenate(
        [
            transposed_times(chosen(pair_one, order), pair_one),
            transposed_times(chosen(pair_up, order), half_up),
        ],
        axis=1,
    ).astype(jnp.bfloat16)
    gram_sum = scatter_blocks(gram_rows.reshape(dp_count, block, model_width + half_width))
    gram_rows = chosen(
        order,
        gather_blocks(gram_sum.astype(jnp.bfloat16)).reshape(model_width, model_width + half_width),
    )
    gram_one = gram_rows[:, :model_width]
    gram_up = gram_rows[:, model_width:]
    gram_up = jnp.concatenate([gram_up, swap(gram_up)], axis=1)
    done_one = schulz(gram_one, pair_one)

    out_padded = jnp.pad(out_rows, ((0, padded_rows - head_rows), (0, 0)))
    out_whole = join(gather_blocks(out_padded).reshape(dp_count * padded_rows, model_width))
    done_out = schulz(
        transposed_times(out_whole, out_whole),
        out_padded,
    )[:head_rows]

    qkv_whole = gather_blocks(jnp.pad(qkv_rows, ((0, -3 * head_rows % 16), (0, 0))))
    qkv_whole = qkv_whole.reshape(-1, model_width)
    gram_qkv = transposed_times(qkv_whole, qkv_whole)
    gram_qkv = gram_qkv + swap(gram_qkv.astype(jnp.bfloat16)).astype(jnp.float32)
    qkv_padded = jnp.pad(qkv_rows, ((0, hidden_rows - 3 * head_rows), (0, 0)))
    pair_two = jnp.where(first_core, pair_up, join(qkv_padded))
    done_two = schulz(jnp.where(first_core, gram_up.astype(jnp.float32), gram_qkv), pair_two)
    returned = swap(jnp.stack([done_one[hidden_rows:], done_two[hidden_rows:]]))
    pieces = (
        jnp.where(first_core, returned[1], done_two[:hidden_rows])[: 3 * head_rows].reshape(
            qkv_weight.shape
        ),
        done_out,
        jnp.where(first_core, done_one[:hidden_rows], returned[0]),
        jnp.where(first_core, done_two[:hidden_rows], returned[1]),
        jnp.where(first_core, returned[0], done_one[:hidden_rows]),
    )
    weights = (qkv_weight, out_weight, gate_weight, up_weight, down_weight)
    row_totals = (3 * D, D, FF, FF, FF)
    updated = [
        weight * (1.0 - ORTHO_RATE * WEIGHT_DECAY)
        - ORTHO_RATE * 0.2 * math.sqrt(row_total) * piece.astype(jnp.float32)
        for weight, piece, row_total in zip(weights, pieces, row_totals)
    ]
    width_part = adam_first.shape[1]
    norm_grad = lax.dynamic_slice_in_dim(norm_totals, dp_index * width_part, width_part, 1)
    norm_now = jnp.concatenate([norm_gains, norm_biases], axis=0)
    norm_first = BETA_FIRST * adam_first + (1.0 - BETA_FIRST) * norm_grad
    norm_second = BETA_SECOND * adam_second + (1.0 - BETA_SECOND) * norm_grad * norm_grad
    first_hat = norm_first / (1.0 - BETA_FIRST**STEP_COUNT)
    second_hat = norm_second / (1.0 - BETA_SECOND**STEP_COUNT)
    norm_updated = norm_now - ADAM_RATE * first_hat / (jnp.sqrt(second_hat) + ADAM_EPSILON)
    return (
        mixed,
        input_grad,
        updated[0],
        updated[1],
        updated[2],
        updated[3],
        updated[4],
        carried[0],
        carried[1],
        carried[2],
        carried[3],
        carried[4],
        norm_updated,
        norm_first,
        norm_second,
    )


def solution(mesh):
    return jax.shard_map(
        on_device,
        mesh=mesh,
        in_specs=(
            P(("dp", "mp"), None),
            P(("dp", "mp"), None),
            P("dp", None),
            P(None, ("mp", "dp"), None),
            P(("mp", "dp"), None),
            P(("mp", "dp"), None),
            P(("mp", "dp"), None),
            P(("mp", "dp"), None),
            P(None, ("mp", "dp"), None),
            P(("mp", "dp"), None),
            P(("mp", "dp"), None),
            P(("mp", "dp"), None),
            P(("mp", "dp"), None),
            P(None, "dp"),
            P(None, "dp"),
            P(None, "dp"),
            P(None, "dp"),
        ),
        out_specs=(
            P(("dp", "mp"), None),
            P(("dp", "mp"), None),
            P(None, ("mp", "dp"), None),
            P(("mp", "dp"), None),
            P(("mp", "dp"), None),
            P(("mp", "dp"), None),
            P(("mp", "dp"), None),
            P(None, ("mp", "dp"), None),
            P(("mp", "dp"), None),
            P(("mp", "dp"), None),
            P(("mp", "dp"), None),
            P(("mp", "dp"), None),
            P(None, "dp"),
            P(None, "dp"),
            P(None, "dp"),
        ),
        check_vma=False,
    )
```

time: 1420 us -> 563 us (0.40)
  waiting for transfers between devices: 729 us -> 181 us
  blocking collectives: 214 us -> 0 us
  matrix products: 317 us -> 145 us
  starting transfers between devices: 62.4 us -> 121 us
  local copies, waits for them, and re-layouts: 20.5 us -> 42.6 us
    all_gather x33 -> x0, waiting for transfers between devices: 393 us -> none  [the longest x1 66.5 us: on_device(): lax.all_gather(rounded_moments[4], 'dp', axis=0, tiled=True)]
    ppermute x0 -> x96, waiting for transfers between devices: none -> 181 us  [the longest x81 181 us: flip(): return lax.ppermute(value, 'dp', [(i, i ^ mask) for i in range(count)])]
    all_gather x8 -> x0, blocking collectives: 176 us -> none  [the longest x1 47.1 us: on_device(): lax.all_gather(shard_list[1], 'dp', axis=0, tiled=True)]
    all_to_all x3 -> x0, waiting for transfers between devices: 171 us -> none  [sum_at_owner(): lax.all_to_all(pieces, axis, split_axis=0, concat_axis=0, tiled=True)]
    reduce_scatter x29 -> x0, waiting for transfers between devices: 160 us -> none  [the longest x5 55.2 us: on_device(): lax.psum_scatter(partial_value[0].astype(jnp.bfloat16), 'mp', scatter_dim...]
    ppermute x0 -> x96, starting transfers between devices: none -> 121 us  [the longest x81 119 us: flip(): return lax.ppermute(value, 'dp', [(i, i ^ mask) for i in range(count)])]
    dot_general x30 -> x10, matrix products: 115 us -> 26 us  [transposed_times(): lax.dot_general(left, right, (((0,), (0,)), ((), ())), preferred_element_...]
    dot_general x30 -> x60, matrix products: 164 us -> 91.8 us  [the longest x12 22.9 us: schulz(): jnp.dot(narrow, narrow, preferred_element_type=jnp.float32)]
  transfers between devices with their start and end apart: 65 -> 96, of which waited for: 52 -> 41; matrix products, arithmetic and copies ran while one was open for 23% -> 37% of each run, Pallas kernels for 0% -> 0%
where the time goes in v1:
time: 563 us; the launch traced here: 553 us
  waiting for transfers between devices  181 us (32%)
  matrix products  145 us (26%)
  starting transfers between devices  121 us (21%)
  other arithmetic  57.2 us (10%)
  local copies, waits for them, and re-layouts  42.6 us (8%)
  between operations  5.69 us (1%)
    ppermute x81, waiting for transfers between devices, flip(): return lax.ppermute(value, 'dp', [(i, i ^ mask) for i in range(count)])  181 us
    ppermute x81, starting transfers between devices, flip(): return lax.ppermute(value, 'dp', [(i, i ^ mask) for i in range(count)])  119 us
    dot_general x10, matrix products, transposed_times(): lax.dot_general(left, right, (((0,), (0,)), ((), ())), preferred_element_...  26 us
    dot_general x12, matrix products, schulz(): jnp.dot(narrow, narrow, preferred_element_type=jnp.float32)  22.9 us
    dot_general x15, matrix products, schulz(): jnp.dot(current, mixing, preferred_element_type=jnp.float32)  21.2 us
    unnamed x235, local copies, waits for them, and re-layouts  19 us
    dot_general x12, matrix products, schulz(): jnp.dot(once.astype(jnp.bfloat16), mixing, preferred_element_type=jnp.flo...  17.8 us
    dot_general x12, matrix products, schulz(): jnp.dot(narrow, mixing, preferred_element_type=jnp.float32)  15.8 us
  transfers between devices with their start and end apart: 96, of which 41 were waited for; matrix products, arithmetic and copies ran while one was open for 37% of the time, Pallas kernels for 0%

profile of v1, /device:TPU:0, one launch (start us, length us, event | category | flops | bytes accessed | tf_op | source)
XLA Modules:
  0.0 552.5 jit_solution(14415458380477572448)
XLA Ops:
  11.8 3.9 collective-permute-start.19
  24.5 4.8 collective-permute-done.18
  29.3 5.6 %collective-permute-start.10 = (bf16[1,192,768]{2,1,0:T(8,128)(2,1)S(1)}, bf16[1,192,768]{2,1,0:T(8,128)(2,1)S(1)}, u32[]{:S(2)}, u32[]{:S(2)}) collective-permute-start(bf16[1,192,768]{2,1,0:T(8,128)(2,1)S(1)} %get-tuple-element.163), channel_id=1, source_target_pairs={{0,8},{2,10},{4,12},{6,14},{8,0},{10,2},{12,4},{14,6},{16,24},{18,... | collective-permute-start | bytes 884744 | tf_op jit(solution)/shard_map/ppermute | solution.py:167
  42.0 4.6 collective-permute-done.10
  48.9 9.7 %collective-permute-done.11 = bf16[1,192,768]{2,1,0:T(8,128)(2,1)S(1)} collective-permute-done((bf16[1,192,768]{2,1,0:T(8,128)(2,1)S(1)}, bf16[1,192,768]{2,1,0:T(8,128)(2,1)S(1)}, u32[]{:S(2)}, u32[]{:S(2)}) %collective-permute-start.11) | collective-permute-done | bytes 294944 | tf_op jit(solution)/shard_map/ppermute | solution.py:167
  67.0 11.4 %collective-permute-done.5 = bf16[4,112,768]{2,1,0:T(8,128)(2,1)S(1)} collective-permute-done((bf16[4,112,768]{2,1,0:T(8,128)(2,1)S(1)}, bf16[4,112,768]{2,1,0:T(8,128)(2,1)S(1)}, u32[]{:S(2)}, u32[]{:S(2)}) %collective-permute-start.5) | collective-permute-done | bytes 688160 | tf_op jit(solution)/shard_map/ppermute | solution.py:167
  81.0 21.8 %collective-permute-done.22 = bf16[4,96,384]{2,1,0:T(8,128)(2,1)S(1)} collective-permute-done((bf16[4,96,384]{2,1,0:T(8,128)(2,1)S(1)}, bf16[4,96,384]{2,1,0:T(8,128)(2,1)S(1)}, u32[]{:S(2)}, u32[]{:S(2)}) %collective-permute-start.22) | collective-permute-done | bytes 294944 | tf_op jit(solution)/shard_map/ppermute | solution.py:167
  114.1 5.4 fusion.278
  119.6 3.8 fusion.37
  138.9 7.3 %collective-permute-done.15 = bf16[4,192,384]{2,1,0:T(8,128)(2,1)S(1)} collective-permute-done((bf16[4,192,384]{2,1,0:T(8,128)(2,1)S(1)}, bf16[4,192,384]{2,1,0:T(8,128)(2,1)S(1)}, u32[]{:S(2)}, u32[]{:S(2)}) %collective-permute-start.15) | collective-permute-done | bytes 589856 | tf_op jit(solution)/shard_map/ppermute | solution.py:167
  172.3 6.1 %multiply_convert_fusion.2 = (bf16[512,1536]{1,0:T(8,128)(2,1)S(1)}, bf16[512,1536]{1,0:T(8,128)(2,1)S(1)}) fusion(f32[512,1536]{1,0:T(8,128)} %copy-done.96, f32[512,1536]{1,0:T(8,128)} %get-tuple-element.192, bf16[1536,768]{1,0:T(8,128)(2,1)} %bitcast.323, bf16[256,768]{1,0:T(8,128)(2,1)} %collective-permute-done.25, bf16[256,768]{1,0:T(8,128)(2,1)} %fusion.248), kind=kOutput, calls=%fused_computation.29 | convolution fusion | flops 1219756032 | bytes 12582912 | tf_op jit(solution)/shard_map/dot_general | solution.py:85
  203.2 21.5 %collective-permute-done.92 = f32[4,768]{1,0:T(4,128)S(1)} collective-permute-done((f32[4,768]{1,0:T(4,128)S(1)}, f32[4,768]{1,0:T(4,128)S(1)}, u32[]{:S(2)}, u32[]{:S(2)}) %collective-permute-start.92) | collective-permute-done | bytes 12320 | tf_op jit(solution)/shard_map/ppermute | solution.py:167
  255.4 3.6 convolution_convert_fusion.7
  305.2 7.5 %collective-permute-done.87 = bf16[4,32,768]{2,1,0:T(8,128)(2,1)S(1)} collective-permute-done((bf16[4,32,768]{2,1,0:T(8,128)(2,1)S(1)}, bf16[4,32,768]{2,1,0:T(8,128)(2,1)S(1)}, u32[]{:S(2)}, u32[]{:S(2)}) %collective-permute-start.87) | collective-permute-done | bytes 196640 | tf_op jit(solution)/shard_map/ppermute | solution.py:167
  328.1 3.6 collective-permute-done.64
  332.5 4.1 collective-permute-start.67
  356.5 18.2 %collective-permute-done.34 = bf16[192,768]{1,0:T(8,128)(2,1)S(1)} collective-permute-done((bf16[192,768]{1,0:T(8,128)(2,1)S(1)}, bf16[192,768]{1,0:T(8,128)(2,1)S(1)}, u32[]{:S(2)}, u32[]{:S(2)}) %collective-permute-start.34) | collective-permute-done | bytes 294944 | tf_op jit(solution)/shard_map/ppermute | solution.py:167
  375.4 7.3 %collective-permute-done.41 = bf16[96,768]{1,0:T(8,128)(2,1)S(1)} collective-permute-done((bf16[96,768]{1,0:T(8,128)(2,1)S(1)}, bf16[96,768]{1,0:T(8,128)(2,1)S(1)}, u32[]{:S(2)}, u32[]{:S(2)}) %collective-permute-start.41) | collective-permute-done | bytes 147488 | tf_op jit(solution)/shard_map/ppermute | solution.py:167
  390.6 4.5 add_convert_fusion.4
  418.2 5.8 %collective-permute-done.46 = bf16[4,48,512]{2,1,0:T(8,128)(2,1)S(1)} collective-permute-done((bf16[4,48,512]{2,1,0:T(8,128)(2,1)S(1)}, bf16[4,48,512]{2,1,0:T(8,128)(2,1)S(1)}, u32[]{:S(2)}, u32[]{:S(2)}) %collective-permute-start.46) | collective-permute-done | bytes 196640 | tf_op jit(solution)/shard_map/ppermute | solution.py:167
  433.2 4.1 collective-permute-done.47
  445.4 4.4 collective-permute-done.49
  457.4 3.5 collective-permute-done.52
  464.2 5.7 %collective-permute-done.54 = bf16[4,48,1152]{2,1,0:T(8,128)(2,1)S(1)} collective-permute-done((bf16[4,48,1152]{2,1,0:T(8,128)(2,1)S(1)}, bf16[4,48,1152]{2,1,0:T(8,128)(2,1)S(1)}, u32[]{:S(2)}, u32[]{:S(2)}) %collective-permute-start.54) | collective-permute-done | bytes 442400 | tf_op jit(solution)/shard_map/ppermute | solution.py:167
  469.9 4.3 collective-permute-start.57
  475.5 4.5 collective-permute-done.56
  485.8 3.6 fusion.12
  508.9 4.8 fusion.48
  513.7 3.8 select_reduce_fusion.1
  518.3 4.5 add_convert_fusion.9
  539.7 4.7 fusion.53
  545.1 4.6 fusion.43
  (653 shorter events, 334.0 us)
Async XLA Ops:
  4.1 30.9 %collective-permute-start.1 = (bf16[1,112,768]{2,1,0:T(8,128)(2,1)S(1)}, bf16[1,112,768]{2,1,0:T(8,128)(2,1)S(1)}, u32[]{:S(2)}, u32[]{:S(2)}) collective-permute-start(bf16[1,112,768]{2,1,0:T(8,128)(2,1)S(1)} %get-tuple-element.170), channel_id=1, source_target_pairs={{0,8},{2,10},{4,12},{6,14},{8,0},{10,2},{12,4},{14,6},{16,24},{18,... | collective-permute-start | bytes 516104 | tf_op jit(solution)/shard_map/ppermute | solution.py:167
  7.1 30.6 %collective-permute-start.2 = (bf16[1,112,768]{2,1,0:T(8,128)(2,1)S(1)}, bf16[1,112,768]{2,1,0:T(8,128)(2,1)S(1)}, u32[]{:S(2)}, u32[]{:S(2)}) collective-permute-start(bf16[1,112,768]{2,1,0:T(8,128)(2,1)S(1)} %get-tuple-element.170), channel_id=1, source_target_pairs={{0,16},{2,18},{4,20},{6,22},{8,24},{10,26},{12,28},{14,30},{16,0},... | collective-permute-start | bytes 516104 | tf_op jit(solution)/shard_map/ppermute | solution.py:167
  29.3 34.9 %collective-permute-start = (bf16[256,768]{1,0:T(8,128)(2,1)S(1)}, bf16[256,768]{1,0:T(8,128)(2,1)S(1)}, u32[]{:S(2)}, u32[]{:S(2)}) collective-permute-start(bf16[256,768]{1,0:T(8,128)(2,1)S(1)} %copy-done.13), channel_id=1, source_target_pairs={{0,1},{1,0},{2,3},{3,2},{4,5},{5,4},{6,7},{7,6},{8,9},{9,8},{10,11... | collective-permute-start | bytes 1179656 | tf_op jit(solution)/shard_map/ppermute | solution.py:162
  35.0 23.5 %collective-permute-start.11 = (bf16[1,192,768]{2,1,0:T(8,128)(2,1)S(1)}, bf16[1,192,768]{2,1,0:T(8,128)(2,1)S(1)}, u32[]{:S(2)}, u32[]{:S(2)}) collective-permute-start(bf16[1,192,768]{2,1,0:T(8,128)(2,1)S(1)} %get-tuple-element.163), channel_id=1, source_target_pairs={{0,16},{2,18},{4,20},{6,22},{8,24},{10,26},{12,28},{14,30},{16,0},... | collective-permute-start | bytes 884744 | tf_op jit(solution)/shard_map/ppermute | solution.py:167
  37.7 22.4 %collective-permute-start.12 = (bf16[1,192,768]{2,1,0:T(8,128)(2,1)S(1)}, bf16[1,192,768]{2,1,0:T(8,128)(2,1)S(1)}, u32[]{:S(2)}, u32[]{:S(2)}) collective-permute-start(bf16[1,192,768]{2,1,0:T(8,128)(2,1)S(1)} %get-tuple-element.163), channel_id=1, source_target_pairs={{0,24},{2,26},{4,28},{6,30},{8,16},{10,18},{12,20},{14,22},{16,8},... | collective-permute-start | bytes 884744 | tf_op jit(solution)/shard_map/ppermute | solution.py:167
  39.8 26.5 %collective-permute-start.20 = (bf16[4,96,768]{2,1,0:T(8,128)(2,1)S(1)}, bf16[4,96,768]{2,1,0:T(8,128)(2,1)S(1)}, u32[]{:S(2)}, u32[]{:S(2)}) collective-permute-start(bf16[4,96,768]{2,1,0:T(8,128)(2,1)S(1)} %pad_maximum_fusion.9), channel_id=1, source_target_pairs={{0,2},{2,0},{4,6},{6,4},{8,10},{10,8},{12,14},{14,12},{16,18},{18,... | collective-permute-start | bytes 1769480 | tf_op jit(solution)/shard_map/ppermute | solution.py:167
  64.1 67.8 %collective-permute-start.13 = (bf16[4,192,768]{2,1,0:T(8,128)(2,1)}, bf16[4,192,768]{2,1,0:T(8,128)(2,1)S(1)}, u32[]{:S(2)}, u32[]{:S(2)}) collective-permute-start(bf16[4,192,768]{2,1,0:T(8,128)(2,1)} %pad_maximum_fusion.1), channel_id=1, source_target_pairs={{0,2},{2,0},{4,6},{6,4},{8,10},{10,8},{12,14},{14,12},{16,18},{18,... | collective-permute-start | bytes 3538952 | tf_op jit(solution)/shard_map/ppermute | solution.py:167
  64.8 38.0 %collective-permute-start.22 = (bf16[4,96,384]{2,1,0:T(8,128)(2,1)S(1)}, bf16[4,96,384]{2,1,0:T(8,128)(2,1)S(1)}, u32[]{:S(2)}, u32[]{:S(2)}) collective-permute-start(bf16[4,96,384]{2,1,0:T(8,128)(2,1)S(1)} %slice.626), channel_id=1, source_target_pairs={{0,2},{2,0},{4,6},{6,4},{8,10},{10,8},{12,14},{14,12},{16,18},{18,... | collective-permute-start | bytes 884744 | tf_op jit(solution)/shard_map/ppermute | solution.py:167
  66.4 37.9 %collective-permute-start.23 = (bf16[4,96,384]{2,1,0:T(8,128)(2,1)S(1)}, bf16[4,96,384]{2,1,0:T(8,128)(2,1)S(1)}, u32[]{:S(2)}, u32[]{:S(2)}) collective-permute-start(bf16[4,96,384]{2,1,0:T(8,128)(2,1)S(1)} %slice.627), channel_id=1, source_target_pairs={{0,4},{2,6},{4,0},{6,2},{8,12},{10,14},{12,8},{14,10},{16,20},{18,... | collective-permute-start | bytes 884744 | tf_op jit(solution)/shard_map/ppermute | solution.py:167
  78.4 28.0 %collective-permute-start.6 = (bf16[4,112,384]{2,1,0:T(8,128)(2,1)S(1)}, bf16[4,112,384]{2,1,0:T(8,128)(2,1)S(1)}, u32[]{:S(2)}, u32[]{:S(2)}) collective-permute-start(bf16[4,112,384]{2,1,0:T(8,128)(2,1)S(1)} %slice.604), channel_id=1, source_target_pairs={{0,2},{2,0},{4,6},{6,4},{8,10},{10,8},{12,14},{14,12},{16,18},{18,... | collective-permute-start | bytes 1032200 | tf_op jit(solution)/shard_map/ppermute | solution.py:167
  79.3 27.2 %collective-permute-start.7 = (bf16[4,112,384]{2,1,0:T(8,128)(2,1)S(1)}, bf16[4,112,384]{2,1,0:T(8,128)(2,1)S(1)}, u32[]{:S(2)}, u32[]{:S(2)}) collective-permute-start(bf16[4,112,384]{2,1,0:T(8,128)(2,1)S(1)} %slice.605), channel_id=1, source_target_pairs={{0,4},{2,6},{4,0},{6,2},{8,12},{10,14},{12,8},{14,10},{16,20},{18,... | collective-permute-start | bytes 1032200 | tf_op jit(solution)/shard_map/ppermute | solution.py:167
  102.8 26.5 %collective-permute-start.14 = (bf16[4,192,768]{2,1,0:T(8,128)(2,1)}, bf16[4,192,768]{2,1,0:T(8,128)(2,1)}, u32[]{:S(2)}, u32[]{:S(2)}) collective-permute-start(bf16[4,192,768]{2,1,0:T(8,128)(2,1)} %pad_maximum_fusion.1), channel_id=1, source_target_pairs={{0,4},{2,6},{4,0},{6,2},{8,12},{10,14},{12,8},{14,10},{16,20},{18,... | collective-permute-start | bytes 3538952 | tf_op jit(solution)/shard_map/ppermute | solution.py:167
  190.6 47.4 %collective-permute-start.29 = (bf16[4,192,384]{2,1,0:T(8,128)(2,1)S(1)}, bf16[4,192,384]{2,1,0:T(8,128)(2,1)S(1)}, u32[]{:S(2)}, u32[]{:S(2)}) collective-permute-start(bf16[4,192,384]{2,1,0:T(8,128)(2,1)S(1)} %get-tuple-element.106), channel_id=1, source_target_pairs={{0,4},{2,6},{4,0},{6,2},{8,12},{10,14},{12,8},{14,10},{16,20},{18,... | collective-permute-start | bytes 1769480 | tf_op jit(solution)/shard_map/ppermute | solution.py:167
  191.2 46.9 %collective-permute-start.31 = (bf16[4,192,384]{2,1,0:T(8,128)(2,1)S(1)}, bf16[4,192,384]{2,1,0:T(8,128)(2,1)S(1)}, u32[]{:S(2)}, u32[]{:S(2)}) collective-permute-start(bf16[4,192,384]{2,1,0:T(8,128)(2,1)S(1)} %get-tuple-element.107), channel_id=1, source_target_pairs={{0,2},{2,0},{4,6},{6,4},{8,10},{10,8},{12,14},{14,12},{16,18},{18,... | collective-permute-start | bytes 1769480 | tf_op jit(solution)/shard_map/ppermute | solution.py:167
  195.7 74.8 %collective-permute-start.37 = (bf16[4,96,768]{2,1,0:T(8,128)(2,1)}, bf16[4,96,768]{2,1,0:T(8,128)(2,1)}, u32[]{:S(2)}, u32[]{:S(2)}) collective-permute-start(bf16[4,96,768]{2,1,0:T(8,128)(2,1)} %pad_maximum_fusion.10), channel_id=1, source_target_pairs={{0,2},{2,0},{4,6},{6,4},{8,10},{10,8},{12,14},{14,12},{16,18},{18,... | collective-permute-start | bytes 1769480 | tf_op jit(solution)/shard_map/ppermute | solution.py:167
  200.0 24.7 %collective-permute-start.92 = (f32[4,768]{1,0:T(4,128)S(1)}, f32[4,768]{1,0:T(4,128)S(1)}, u32[]{:S(2)}, u32[]{:S(2)}) collective-permute-start(f32[4,768]{1,0:T(4,128)S(1)} %fusion.245), channel_id=1, source_target_pairs={{0,2},{2,0},{4,6},{6,4},{8,10},{10,8},{12,14},{14,12},{16,18},{18,... | collective-permute-start | bytes 36872 | tf_op jit(solution)/shard_map/ppermute | solution.py:167
  201.7 70.4 %collective-permute-start.39 = (bf16[4,96,768]{2,1,0:T(8,128)(2,1)}, bf16[4,96,768]{2,1,0:T(8,128)(2,1)}, u32[]{:S(2)}, u32[]{:S(2)}) collective-permute-start(bf16[4,96,768]{2,1,0:T(8,128)(2,1)} %pad_maximum_fusion.11), channel_id=1, source_target_pairs={{0,4},{2,6},{4,0},{6,2},{8,12},{10,14},{12,8},{14,10},{16,20},{18,... | collective-permute-start | bytes 1769480 | tf_op jit(solution)/shard_map/ppermute | solution.py:167
  239.5 100.0 %collective-permute-start.30 = (bf16[4,192,768]{2,1,0:T(8,128)(2,1)}, bf16[4,192,768]{2,1,0:T(8,128)(2,1)}, u32[]{:S(2)}, u32[]{:S(2)}) collective-permute-start(bf16[4,192,768]{2,1,0:T(8,128)(2,1)} %pad_maximum_fusion.2), channel_id=1, source_target_pairs={{0,2},{2,0},{4,6},{6,4},{8,10},{10,8},{12,14},{14,12},{16,18},{18,... | collective-permute-start | bytes 3538952 | tf_op jit(solution)/shard_map/ppermute | solution.py:167
  275.2 27.3 %collective-permute-start.28 = (bf16[256,768]{1,0:T(8,128)(2,1)S(1)}, bf16[256,768]{1,0:T(8,128)(2,1)S(1)}, u32[]{:S(2)}, u32[]{:S(2)}) collective-permute-start(bf16[256,768]{1,0:T(8,128)(2,1)S(1)} %slice.1030), channel_id=1, source_target_pairs={{0,1},{1,0},{2,3},{3,2},{4,5},{5,4},{6,7},{7,6},{8,9},{9,8},{10,11... | collective-permute-start | bytes 1179656 | tf_op jit(solution)/shard_map/ppermute | solution.py:162
  297.3 23.3 %collective-permute-start.59 = (bf16[4,80,768]{2,1,0:T(8,128)(2,1)S(1)}, bf16[4,80,768]{2,1,0:T(8,128)(2,1)S(1)}, u32[]{:S(2)}, u32[]{:S(2)}) collective-permute-start(bf16[4,80,768]{2,1,0:T(8,128)(2,1)S(1)} %pad_maximum_fusion.16), channel_id=1, source_target_pairs={{0,2},{2,0},{4,6},{6,4},{8,10},{10,8},{12,14},{14,12},{16,18},{18,... | collective-permute-start | bytes 1474568 | tf_op jit(solution)/shard_map/ppermute | solution.py:167
  298.5 22.0 %collective-permute-start.61 = (bf16[4,80,768]{2,1,0:T(8,128)(2,1)S(1)}, bf16[4,80,768]{2,1,0:T(8,128)(2,1)S(1)}, u32[]{:S(2)}, u32[]{:S(2)}) collective-permute-start(bf16[4,80,768]{2,1,0:T(8,128)(2,1)S(1)} %fusion.157), channel_id=1, source_target_pairs={{0,4},{2,6},{4,0},{6,2},{8,12},{10,14},{12,8},{14,10},{16,20},{18,... | collective-permute-start | bytes 1474568 | tf_op jit(solution)/shard_map/ppermute | solution.py:167
  317.3 24.2 %collective-permute-start.32 = (bf16[4,192,768]{2,1,0:T(8,128)(2,1)S(1)}, bf16[4,192,768]{2,1,0:T(8,128)(2,1)S(1)}, u32[]{:S(2)}, u32[]{:S(2)}) collective-permute-start(bf16[4,192,768]{2,1,0:T(8,128)(2,1)S(1)} %copy-done.19), channel_id=1, source_target_pairs={{0,4},{2,6},{4,0},{6,2},{8,12},{10,14},{12,8},{14,10},{16,20},{18,... | collective-permute-start | bytes 3538952 | tf_op jit(solution)/shard_map/ppermute | solution.py:167
  325.8 49.5 %collective-permute-start.40 = (bf16[96,768]{1,0:T(8,128)(2,1)S(1)}, bf16[96,768]{1,0:T(8,128)(2,1)S(1)}, u32[]{:S(2)}, u32[]{:S(2)}) collective-permute-start(bf16[96,768]{1,0:T(8,128)(2,1)S(1)} %get-tuple-element.147), channel_id=1, source_target_pairs={{0,8},{2,10},{4,12},{6,14},{8,0},{10,2},{12,4},{14,6},{16,24},{18,... | collective-permute-start | bytes 442376 | tf_op jit(solution)/shard_map/ppermute | solution.py:167
  343.5 31.2 %collective-permute-start.34 = (bf16[192,768]{1,0:T(8,128)(2,1)S(1)}, bf16[192,768]{1,0:T(8,128)(2,1)S(1)}, u32[]{:S(2)}, u32[]{:S(2)}) collective-permute-start(bf16[192,768]{1,0:T(8,128)(2,1)S(1)} %get-tuple-element.131), channel_id=1, source_target_pairs={{0,16},{2,18},{4,20},{6,22},{8,24},{10,26},{12,28},{14,30},{16,0},... | collective-permute-start | bytes 884744 | tf_op jit(solution)/shard_map/ppermute | solution.py:167
  346.6 28.1 %collective-permute-start.35 = (bf16[192,768]{1,0:T(8,128)(2,1)S(1)}, bf16[192,768]{1,0:T(8,128)(2,1)S(1)}, u32[]{:S(2)}, u32[]{:S(2)}) collective-permute-start(bf16[192,768]{1,0:T(8,128)(2,1)S(1)} %get-tuple-element.130), channel_id=1, source_target_pairs={{0,24},{2,26},{4,28},{6,30},{8,16},{10,18},{12,20},{14,22},{16,8},... | collective-permute-start | bytes 884744 | tf_op jit(solution)/shard_map/ppermute | solution.py:167
  349.8 32.8 %collective-permute-start.41 = (bf16[96,768]{1,0:T(8,128)(2,1)S(1)}, bf16[96,768]{1,0:T(8,128)(2,1)S(1)}, u32[]{:S(2)}, u32[]{:S(2)}) collective-permute-start(bf16[96,768]{1,0:T(8,128)(2,1)S(1)} %get-tuple-element.149), channel_id=1, source_target_pairs={{0,16},{2,18},{4,20},{6,22},{8,24},{10,26},{12,28},{14,30},{16,0},... | collective-permute-start | bytes 442376 | tf_op jit(solution)/shard_map/ppermute | solution.py:167
  354.6 30.0 %collective-permute-start.42 = (bf16[96,768]{1,0:T(8,128)(2,1)S(1)}, bf16[96,768]{1,0:T(8,128)(2,1)S(1)}, u32[]{:S(2)}, u32[]{:S(2)}) collective-permute-start(bf16[96,768]{1,0:T(8,128)(2,1)S(1)} %get-tuple-element.148), channel_id=1, source_target_pairs={{0,24},{2,26},{4,28},{6,30},{8,16},{10,18},{12,20},{14,22},{16,8},... | collective-permute-start | bytes 442376 | tf_op jit(solution)/shard_map/ppermute | solution.py:167
  374.7 162.2 %collective-permute-start.65 = (bf16[96,768]{1,0:T(8,128)(2,1)}, bf16[96,768]{1,0:T(8,128)(2,1)}, u32[]{:S(2)}, u32[]{:S(2)}) collective-permute-start(bf16[96,768]{1,0:T(8,128)(2,1)} %pad.24), channel_id=1, source_target_pairs={{0,1},{1,0},{2,3},{3,2},{4,5},{5,4},{6,7},{7,6},{8,9},{9,8},{10,11... | collective-permute-start | bytes 442376 | tf_op jit(solution)/shard_map/ppermute | solution.py:162
  375.3 54.3 %collective-permute-start.70 = (bf16[4,80,768]{2,1,0:T(8,128)(2,1)}, bf16[4,80,768]{2,1,0:T(8,128)(2,1)}, u32[]{:S(2)}, u32[]{:S(2)}) collective-permute-start(bf16[4,80,768]{2,1,0:T(8,128)(2,1)} %pad_maximum_fusion.17), channel_id=1, source_target_pairs={{0,2},{2,0},{4,6},{6,4},{8,10},{10,8},{12,14},{14,12},{16,18},{18,... | collective-permute-start | bytes 1474568 | tf_op jit(solution)/shard_map/ppermute | solution.py:167
  382.7 45.3 %collective-permute-start.71 = (bf16[4,80,768]{2,1,0:T(8,128)(2,1)}, bf16[4,80,768]{2,1,0:T(8,128)(2,1)}, u32[]{:S(2)}, u32[]{:S(2)}) collective-permute-start(bf16[4,80,768]{2,1,0:T(8,128)(2,1)} %pad_maximum_fusion.17), channel_id=1, source_target_pairs={{0,4},{2,6},{4,0},{6,2},{8,12},{10,14},{12,8},{14,10},{16,20},{18,... | collective-permute-start | bytes 1474568 | tf_op jit(solution)/shard_map/ppermute | solution.py:167
  386.3 24.4 %collective-permute-start.43 = (bf16[2,96,768]{2,1,0:T(8,128)(2,1)S(1)}, bf16[2,96,768]{2,1,0:T(8,128)(2,1)S(1)}, u32[]{:S(2)}, u32[]{:S(2)}) collective-permute-start(bf16[2,96,768]{2,1,0:T(8,128)(2,1)S(1)} %pad_maximum_fusion.28), channel_id=1, source_target_pairs={{0,1},{1,0},{2,3},{3,2},{4,5},{5,4},{6,7},{7,6},{8,9},{9,8},{10,11... | collective-permute-start | bytes 884744 | tf_op jit(solution)/shard_map/ppermute | solution.py:162
  457.2 56.6 %collective-permute-start.74 = (bf16[768,768]{1,0:T(8,128)(2,1)}, bf16[768,768]{1,0:T(8,128)(2,1)}, u32[]{:S(2)}, u32[]{:S(2)}) collective-permute-start(bf16[768,768]{1,0:T(8,128)(2,1)} %get-tuple-element.195), channel_id=1, source_target_pairs={{0,1},{1,0},{2,3},{3,2},{4,5},{5,4},{6,7},{7,6},{8,9},{9,8},{10,11... | collective-permute-start | bytes 3538952 | tf_op jit(solution)/shard_map/ppermute | solution.py:162
  (165 other events, 1731.6 us)
